TPU v7x, 32 devices: a whole 2x2x4 slice. The times are simulated.
32 devices in a mesh: groups: 2 (over y), expert: 4 (over z), dp: 2 (over x), head: 2 (over core).
Axes of the slice: x: 2, y: 2, z: 4, core: 2. Of those that a mesh axis runs over, the one named last changes fastest.
Arguments:
- hidden: bfloat16 [4, 1024, 1536], P(('groups', 'dp'), ('expert', 'head')), parts along dimension 0, may hold values from -6 to 6
- modulation: float32 [4, 3, 1536], P(('groups', 'dp')), parts along dimension 0, may hold values from -3 to 3
- router_weight: float32 [1536, 16], replicated, may hold values from -0.15625 to 0.15625
- route_ids: int32 [4, 1024, 2], P(('groups', 'dp'), ('expert', 'head')), parts along dimension 0, may hold values from 0 to 15, all different within a row; in each aligned block of 128 rows (0 to 127, 128 to 255, ..., all dimensions but the last counted through in order) at most 32 rows name the same one
- gate_weight: bfloat16 [1536, 98304], P(None, ('expert', 'dp', 'head')), may hold values from -0.15625 to 0.15625
- up_weight: bfloat16 [1536, 98304], P(None, ('expert', 'dp', 'head')), may hold values from -0.15625 to 0.15625
- down_weight: bfloat16 [98304, 1536], P(('expert', 'dp', 'head')), may hold values from -0.078125 to 0.078125
- main_final: bfloat16 [1536, 16], replicated, may hold values from -0.15625 to 0.15625
- guide_qkv: bfloat16 [4, 1024, 6, 192], P(('groups', 'dp'), 'expert', 'head'), parts along dimension 0, may hold values from -6 to 6
- guide_out: bfloat16 [6, 64, 384], P('head'), may hold values from -0.3125 to 0.3125
- guide_final: bfloat16 [384, 16], replicated, may hold values from -0.3125 to 0.3125
- latent: float32 [4, 1024, 16], P(('groups', 'dp'), ('expert', 'head')), parts along dimension 0, may hold values from -6 to 6
- guidance: float32 [4], P(('groups', 'dp')), parts along dimension 0, may hold values from 1.5 to 3
- step_size: float32 [4], P(('groups', 'dp')), parts along dimension 0, may hold values from 0.1 to 0.5
Outputs:
- next_latent: float32 [4, 1024, 16], P(('groups', 'dp'), ('expert', 'head')), parts along dimension 0
There are 2 independent parts, one for each index of `groups`. A program takes and returns all parts, laid end to end along the dimension named above; an argument that names none is the same for every part. Nothing has to cross between parts.
Inputs may be any that keep to these rules, and one draw needn't show every extreme that they name: `route_ids`: each token names 2 different experts. In each aligned block of 128 tokens of a latent (tokens 128 j to 128 (j + 1) - 1), no expert is named by more than 32 routes, a bound that some block reaches.
All inputs are finite; a program needn't handle non-finite values.
Results may differ from a plain program's by a relative error of at most 0.0065.
Values may be sent and summed in bfloat16 or wider, within the bound.
A program may use at most 192 MiB of HBM per device.

v0:
```python
import jax
import jax.numpy as jnp
from jax import lax
from jax.sharding import PartitionSpec as P

FF = 6144
EXPERTS = 16
TOP = 2
HD = 64
P_SIZE = 16


epsilon = 1e-06
score_scale = 8.0


def layer_norm(values):
    average = jnp.mean(values, axis=-1, keepdims=True)
    centered = values - average
    return centered / jnp.sqrt(jnp.mean(centered * centered, axis=-1, keepdims=True) + epsilon)


def unit_rows(values):
    return values / jnp.sqrt(jnp.mean(values * values, axis=-1, keepdims=True) + epsilon)


def route_slots(flat_ids, block_slots, per_index, copies):
    route_flat = flat_ids.reshape(-1)
    one_hot = (route_flat[:, None] == jnp.arange(EXPERTS, dtype=jnp.int32)[None, :]).astype(
        jnp.int32
    )
    earlier = jnp.cumsum(one_hot, axis=0) - one_hot
    earlier_count = jnp.sum(earlier * one_hot, axis=1)
    slot_pos = route_flat % per_index * block_slots + earlier_count
    targets = (
        route_flat[:, None] * copies + jnp.arange(copies, dtype=jnp.int32)[None, :]
    ) // per_index
    return (targets, slot_pos)


def expert_hidden(
    rows, positions, gate_weight, up_weight, my_expert, index_first, block_slots, copies
):
    owner_expert = (index_first + positions // block_slots) // copies
    keep_mask = (owner_expert == my_expert).astype(jnp.float32)[:, None]
    gate_vals = jnp.dot(rows, gate_weight, preferred_element_type=jnp.float32)
    up_vals = jnp.dot(rows, up_weight, preferred_element_type=jnp.float32)
    return (jax.nn.silu(gate_vals) * up_vals * keep_mask).astype(jnp.bfloat16)


def body(
    hidden,
    modulation,
    router_weight,
    route_ids,
    gate_weight,
    up_weight,
    down_weight,
    main_final,
    guide_qkv,
    guide_out,
    guide_final,
    latent,
    guidance,
    step_size,
):
    lat_dev, tok_dev, width = hidden.shape
    experts_axis = lax.axis_size("expert")
    group_size = lax.axis_size(("dp", "head"))
    slice_units = gate_weight.shape[1]
    index_units = slice_units * group_size
    if EXPERTS >= experts_axis:
        per_index = EXPERTS // experts_axis
        copies = 1
    else:
        per_index = 1
        copies = experts_axis // EXPERTS
    capacity = max(2, 2 * tok_dev * TOP // EXPERTS)
    block_slots = lat_dev * capacity
    slot_count = per_index * block_slots
    my_index = lax.axis_index("expert")
    my_member = lax.axis_index(("dp", "head"))
    my_expert = (my_index * index_units + my_member * slice_units) // FF
    index_first = my_index * per_index
    hidden_float = hidden.astype(jnp.float32)
    modulated = (
        layer_norm(hidden_float) * (1.0 + modulation[:, 1][:, None, :])
        + modulation[:, 0][:, None, :]
    ).astype(jnp.bfloat16)
    row_count = lat_dev * tok_dev
    flat_rows = modulated.reshape(row_count, width)
    logits = jnp.dot(flat_rows.astype(jnp.float32), router_weight, precision=lax.Precision.HIGHEST)
    flat_ids = route_ids.reshape(row_count, TOP)
    picked = jnp.take_along_axis(logits, flat_ids, axis=1)
    first_weight = jax.nn.sigmoid(picked[:, 0] - picked[:, 1])
    route_weight = jnp.stack([first_weight, 1.0 - first_weight], axis=1)
    route_count = row_count * TOP
    route_token = jnp.arange(route_count, dtype=jnp.int32) // TOP
    targets, slot_pos = route_slots(flat_ids, block_slots, per_index, copies)
    outgoing = jnp.zeros((experts_axis, slot_count, width), jnp.bfloat16)
    payload = jnp.broadcast_to(flat_rows[route_token][:, None, :], (route_count, copies, width))
    outgoing = outgoing.at[targets, slot_pos[:, None]].set(payload)
    received = lax.all_to_all(outgoing, "expert", split_axis=0, concat_axis=0, tiled=True)
    received_rows = received.reshape(experts_axis * slot_count, width)
    piece = lax.all_gather(received_rows, ("dp", "head"), axis=0, tiled=True)
    positions = jnp.arange(piece.shape[0], dtype=jnp.int32) % slot_count
    activated = expert_hidden(
        piece, positions, gate_weight, up_weight, my_expert, index_first, block_slots, copies
    )
    term = jnp.dot(activated, down_weight, preferred_element_type=jnp.float32)
    row_sums = lax.psum_scatter(
        lax.optimization_barrier(term.astype(jnp.bfloat16))
        .astype(jnp.float32)
        .astype(jnp.bfloat16),
        ("dp", "head"),
        scatter_dimension=0,
        tiled=True,
    ).astype(jnp.float32)
    returned = lax.all_to_all(
        row_sums.reshape(experts_axis, slot_count, width).astype(jnp.bfloat16),
        "expert",
        split_axis=0,
        concat_axis=0,
        tiled=True,
    ).astype(jnp.float32)
    gathered_back = returned[targets, slot_pos[:, None]]
    per_route = jnp.sum(gathered_back, axis=1).reshape(row_count, TOP, width)
    moe_out = jnp.sum(per_route * route_weight[:, :, None], axis=1)
    updated = hidden_float + modulation[:, 2][:, None, :] * moe_out.reshape(lat_dev, tok_dev, width)
    main_norm = layer_norm(updated).astype(jnp.bfloat16)
    main_velocity = jnp.dot(
        main_norm.reshape(row_count, width), main_final, preferred_element_type=jnp.float32
    ).reshape(lat_dev, tok_dev, P_SIZE)
    queries = unit_rows(guide_qkv[..., :HD].astype(jnp.float32)).astype(jnp.bfloat16)
    unit_keys = unit_rows(guide_qkv[..., HD : 2 * HD].astype(jnp.float32)).astype(jnp.bfloat16)
    key_value = jnp.concatenate([unit_keys, guide_qkv[..., 2 * HD :]], axis=-1)
    piece = lax.all_gather(key_value, "expert", axis=1, tiled=True)
    key_piece = piece[..., :HD]
    value_piece = piece[..., HD:]
    scores = jnp.einsum(
        "lqhc,lkhc->lhqk", queries, key_piece, preferred_element_type=jnp.float32
    ) * (score_scale / HD)
    weights = jnp.exp(scores - score_scale)
    weighted_sum = jnp.einsum(
        "lhqk,lkhc->lqhc",
        weights.astype(jnp.bfloat16),
        value_piece,
        preferred_element_type=jnp.float32,
    )
    weight_total = jnp.transpose(jnp.sum(weights, axis=-1), (0, 2, 1))
    weighted_sum, weight_total = (weighted_sum, weight_total)
    attended = (weighted_sum / weight_total[..., None]).astype(jnp.bfloat16)
    partial_mix = jnp.einsum(
        "lqhc,hcd->lqd", attended, guide_out, preferred_element_type=jnp.float32
    )
    guide_mix = lax.psum_scatter(
        partial_mix.astype(jnp.bfloat16), "head", scatter_dimension=1, tiled=True
    ).astype(jnp.float32)
    guide_norm = layer_norm(guide_mix).astype(jnp.bfloat16)
    guide_width = guide_norm.shape[-1]
    guide_velocity = jnp.dot(
        guide_norm.reshape(row_count, guide_width), guide_final, preferred_element_type=jnp.float32
    ).reshape(lat_dev, tok_dev, P_SIZE)
    guided = guide_velocity + guidance[:, None, None] * (main_velocity - guide_velocity)
    return latent + step_size[:, None, None] * guided


def solution(mesh):
    in_specs = (
        P(("groups", "dp"), ("expert", "head"), None),
        P(("groups", "dp"), None, None),
        P(),
        P(("groups", "dp"), ("expert", "head"), None),
        P(None, ("expert", "dp", "head")),
        P(None, ("expert", "dp", "head")),
        P(("expert", "dp", "head"), None),
        P(),
        P(("groups", "dp"), "expert", "head", None),
        P("head", None, None),
        P(),
        P(("groups", "dp"), ("expert", "head"), None),
        P(("groups", "dp")),
        P(("groups", "dp")),
    )
    out_specs = P(("groups", "dp"), ("expert", "head"), None)
    return jax.shard_map(body, mesh=mesh, in_specs=in_specs, out_specs=out_specs, check_vma=False)
```

profile of v0, /device:TPU:13, one launch (start us, length us, event | category | flops | bytes accessed | tf_op | source)
XLA Modules:
  0.0 390.8 jit_solution(16349027691568316379)
XLA Ops:
  8.6 1.1 convert_reduce_fusion
  9.8 1.2 fusion.27
  11.0 1.4 slice_reduce_fusion.2
  13.9 1.2 fusion.33
  15.2 1.3 gather_fusion
  16.6 19.7 %scatter_fusion = bf16[4,128,1536]{2,1,0:T(8,128)(2,1)S(1)} fusion(bf16[4,128,1536]{2,1,0:T(8,128)(2,1)S(1)} %broadcast_in_dim.8, s32[256]{0:T(256)S(1)} %bitcast.123, bf16[256,1536]{1,0:T(8,128)(2,1)S(1)} %gather_fusion), kind=kCustom, calls=%fused_computation.3 | custom fusion | bytes 2361344 | tf_op jit(solution)/shard_map/scatter | solution.py:102
  36.3 38.9 %all_to_all.10 = bf16[4,128,1536]{2,1,0:T(8,128)(2,1)} all-to-all(bf16[4,128,1536]{2,1,0:T(8,128)(2,1)S(1)} %scatter_fusion), channel_id=1, replica_groups=mesh['groups'=2,'expert'=4,'dp'=2,'head'=2] {'expert'}, dimensions={0} | all-to-all | bytes 3145728 | tf_op jit(solution)/shard_map/all_to_all | solution.py:103
  75.3 48.7 %all-gather.2.cloned.1.call-done = bf16[2048,1536]{1,0:T(8,128)(2,1)} async-done(((bf16[512,1536]{1,0:T(8,128)(2,1)}), bf16[2048,1536]{1,0:T(8,128)(2,1)}) %all-gather.2.cloned.1.call-update) | async-done | bytes 6291472 | tf_op jit(solution)/shard_map/all_gather | solution.py:105
  124.0 47.5 %fusion.78 = f32[2048,6144]{1,0:T(8,128)} fusion(bf16[2048,1536]{1,0:T(8,128)(2,1)} %all-gather.2.cloned.1.call-done, bf16[1536,6144]{1,0:T(8,128)(2,1)} %param.18), kind=kOutput, calls=%fused_computation.133 | convolution fusion | flops 38654705664 | bytes 75497472 | tf_op jit(solution)/shard_map/dot_general | solution.py:46
  171.5 55.4 %multiply_convert_fusion.clone.4 = bf16[2048,6144]{1,0:T(8,128)(2,1)} fusion(f32[2048,6144]{1,0:T(8,128)} %fusion.78, bf16[2048,1536]{1,0:T(8,128)(2,1)} %all-gather.2.cloned.1.call-done, bf16[1536,6144]{1,0:T(8,128)(2,1)} %param.19, f32[2048]{0:T(1024)S(1)} %fusion.63), kind=kOutput, calls=%fused_computation.4.clone.clone.clone.1 | convolution fusion | flops 38742786048 | bytes 100671488 | tf_op jit(solution)/shard_map/dot_general | solution.py:47
  226.9 48.0 %convolution_convert_fusion = bf16[2048,1536]{1,0:T(8,128)(2,1)} fusion(bf16[6144,1536]{1,0:T(8,128)(2,1)} %param.20, bf16[2048,6144]{1,0:T(8,128)(2,1)} %multiply_convert_fusion.clone.4), kind=kOutput, calls=%fused_computation.5 | convolution fusion | flops 38657851392 | bytes 50331648 | tf_op jit(solution)/shard_map/dot_general | solution.py:110
  276.1 16.8 %all_gather.6 = bf16[1,1024,3,128]{1,3,2,0:T(8,128)(2,1)S(1)} all-gather(bf16[1,256,3,128]{1,3,2,0:T(8,128)(2,1)S(1)} %pad_maximum_fusion), channel_id=1, replica_groups=mesh['groups'=2,'expert'=4,'dp'=2,'head'=2] {'expert'}, dimensions={1}, use_global_device_ids=true | all-gather | bytes 983040 | tf_op jit(solution)/shard_map/all_gather | solution.py:137
  292.9 40.2 %reduce-scatter.5.cloned.1.call-done = bf16[512,1536]{1,0:T(8,128)(2,1)} async-done(((bf16[2048,1536]{1,0:T(8,128)(2,1)}), bf16[512,1536]{1,0:T(8,128)(2,1)}) %reduce-scatter.5.cloned.1.call-update) | async-done | bytes 1572880 | tf_op jit(solution)/shard_map/reduce_scatter | solution.py:111
  333.1 4.6 %all-to-all-start.1 = ((bf16[4,128,1536]{2,1,0:T(8,128)(2,1)}), bf16[4,128,1536]{2,1,0:T(8,128)(2,1)}, u32[]{:S(2)}, u32[]{:S(2)}) async-start(bf16[4,128,1536]{2,1,0:T(8,128)(2,1)} %bitcast.125), calls=%async_computation.3 | async-start | bytes 3145728 | tf_op jit(solution)/shard_map/all_to_all | solution.py:119
  337.7 2.4 fusion
  340.1 3.6 fusion.7
  344.4 2.3 gather_fusion.2
  348.3 4.3 %reduce-scatter.3.cloned.1.call-done = bf16[1,128,384]{2,1,0:T(8,128)(2,1)} async-done(((bf16[1,256,384]{2,1,0:T(8,128)(2,1)}), bf16[1,128,384]{2,1,0:T(8,128)(2,1)}) %reduce-scatter.3.cloned.1.call-update) | async-done | bytes 98320 | tf_op jit(solution)/shard_map/reduce_scatter | solution.py:156
  355.8 14.9 %all-to-all-done.1 = bf16[4,128,1536]{2,1,0:T(8,128)(2,1)} async-done(((bf16[4,128,1536]{2,1,0:T(8,128)(2,1)}), bf16[4,128,1536]{2,1,0:T(8,128)(2,1)}, u32[]{:S(2)}, u32[]{:S(2)}) %all-to-all-start.1) | async-done | bytes 1572896 | tf_op jit(solution)/shard_map/all_to_all | solution.py:119
  370.7 1.8 convert_element_type.89
  372.6 4.0 %gather_fusion.1 = f32[256,1536]{1,0:T(8,128)} fusion(f32[4,128,1536]{2,1,0:T(8,128)S(1)} %convert_element_type.89, s32[256]{0:T(256)S(1)} %bitcast.122), kind=kCustom, calls=%fused_computation.1 | custom fusion | bytes 3147776 | tf_op jit(solution)/shard_map/gather | solution.py:126
  376.5 2.3 reshape.505
  378.8 2.2 multiply_reduce_fusion
  381.0 1.2 fusion.38
  (75 shorter events, 9.5 us)
Async XLA Ops:
  7.4 332.7 %copy-start = (bf16[3,64,384]{2,1,0:T(8,128)(2,1)S(1)}, bf16[3,64,384]{2,1,0:T(8,128)(2,1)}, u32[]{:S(2)}) copy-start(bf16[3,64,384]{2,1,0:T(8,128)(2,1)} %param.23) | copy-start | bytes 442372
  7.4 116.6 %all-gather.2.cloned.1.call-start = ((), (), s32[]{:S(2)}) async-start(), calls=%async_computation.5 | async-start | bytes 7864320 | tf_op jit(solution)/shard_map/all_gather | solution.py:105
  15.2 21.1 %copy-start.1 = (bf16[128,1536]{1,0:T(8,128)(2,1)}, bf16[128,1536]{1,0:T(8,128)(2,1)S(1)}, u32[]{:S(2)}) copy-start(bf16[128,1536]{1,0:T(8,128)(2,1)S(1)} %fusion.33) | copy-start | bytes 1179652
  75.2 257.9 %reduce-scatter.5.cloned.1.call-start = ((), (), s32[]{:S(2)}) async-start(), calls=%async_computation.6 | async-start | bytes 7864320 | tf_op jit(solution)/shard_map/reduce_scatter | solution.py:111
  274.9 1.0 copy-start.5
  274.9 1.1 slice-start
  276.1 67.6 %copy-start.8 = (s32[1,128,2]{1,2,0:T(2,128)S(1)}, s32[1,128,2]{1,2,0:T(2,128)}, u32[]{:S(2)}) copy-start(s32[1,128,2]{1,2,0:T(2,128)} %param.17) | copy-start | bytes 3076
  276.1 67.9 %copy-start.2 = (bf16[128,1536]{1,0:T(8,128)(2,1)S(1)}, bf16[128,1536]{1,0:T(8,128)(2,1)}, u32[]{:S(2)}) copy-start(bf16[128,1536]{1,0:T(8,128)(2,1)} %copy-done.1) | copy-start | bytes 1179652
  276.1 67.9 %copy-start.6 = (f32[1536,16]{0,1:T(8,128)S(1)}, f32[1536,16]{0,1:T(8,128)}, u32[]{:S(2)}) copy-start(f32[1536,16]{0,1:T(8,128)} %param.16) | copy-start | bytes 294916
  333.1 37.6 %all-to-all-start.1 = ((bf16[4,128,1536]{2,1,0:T(8,128)(2,1)}), bf16[4,128,1536]{2,1,0:T(8,128)(2,1)}, u32[]{:S(2)}, u32[]{:S(2)}) async-start(bf16[4,128,1536]{2,1,0:T(8,128)(2,1)} %bitcast.125), calls=%async_computation.3 | async-start | bytes 3145728 | tf_op jit(solution)/shard_map/all_to_all | solution.py:119
  337.7 14.9 %reduce-scatter.3.cloned.1.call-start = ((), (), s32[]{:S(2)}) async-start(), calls=%async_computation.4 | async-start | bytes 294912 | tf_op jit(solution)/shard_map/reduce_scatter | solution.py:156
  344.4 10.3 %copy-start.10 = (bf16[384,16]{0,1:T(8,128)(2,1)S(1)}, bf16[384,16]{0,1:T(8,128)(2,1)}, u32[]{:S(2)}) copy-start(bf16[384,16]{0,1:T(8,128)(2,1)} %param.24) | copy-start | bytes 36868
  344.4 28.2 %copy-start.3 = (s32[256,1]{0,1:T(1,128)S(1)}, s32[256,1]{0,1:T(1,128)}, u32[]{:S(2)}) copy-start(s32[256,1]{0,1:T(1,128)} %get-tuple-element.13) | copy-start | bytes 3076
  372.5 8.4 %copy-start.7 = (f32[1536]{0:T(1024)S(1)}, f32[1536]{0:T(1024)}, u32[]{:S(2)}) copy-start(f32[1536]{0:T(1024)} %get-tuple-element.7) | copy-start | bytes 18436
  376.5 5.7 %copy-start.4 = (bf16[1,128,1536]{2,1,0:T(8,128)(2,1)S(1)}, bf16[1,128,1536]{2,1,0:T(8,128)(2,1)}, u32[]{:S(2)}) copy-start(bf16[1,128,1536]{2,1,0:T(8,128)(2,1)} %param.14) | copy-start | bytes 1179652
  376.5 5.9 %copy-start.9 = (bf16[1536,16]{0,1:T(8,128)(2,1)S(1)}, bf16[1536,16]{0,1:T(8,128)(2,1)}, u32[]{:S(2)}) copy-start(bf16[1536,16]{0,1:T(8,128)(2,1)} %param.21) | copy-start | bytes 147460
  376.5 5.9 %copy-start.11 = (f32[1,128,16]{1,2,0:T(8,128)S(1)}, f32[1,128,16]{1,2,0:T(8,128)}, u32[]{:S(2)}) copy-start(f32[1,128,16]{1,2,0:T(8,128)} %param.25) | copy-start | bytes 24580
Sparse Core Ops, SparseCore 0:
  75.3 48.6 all-gather.1
  275.1 57.9 reduce-scatter.4
Sparse Core Ops, SparseCore 1:
  343.8 8.8 reduce-scatter.2
where the time goes:
time: 397 us; the launch traced here: 391 us
  matrix products  159 us (40%)
  waiting for transfers between devices  108 us (27%)
  blocking collectives  55.7 us (14%)
  local copies, waits for them, and re-layouts  32.5 us (8%)
  between operations  16.5 us (4%)
  other arithmetic  14 us (4%)
  starting transfers between devices  4.63 us (1%)
    dot_general x1, matrix products, expert_hidden(): up_vals = jnp.dot(rows, up_weight, preferred_element_type=jnp.float32)  55.4 us
    all_gather x1, waiting for transfers between devices, body(): piece = lax.all_gather(received_rows, ('dp', 'head'), axis=0, tiled=True)  48.7 us
    dot_general x1, matrix products, body(): term = jnp.dot(activated, down_weight, preferred_element_type=jnp.float32)  48 us
    dot_general x1, matrix products, expert_hidden(): gate_vals = jnp.dot(rows, gate_weight, preferred_element_type=jnp.float32)  47.5 us
    reduce_scatter x1, waiting for transfers between devices, body(): lax.psum_scatter(lax.optimization_barrier(term.astype(jnp.bfloat16)).asty...  40.2 us
    all_to_all x1, blocking collectives, body(): lax.all_to_all(outgoing, 'expert', split_axis=0, concat_axis=0, tiled=True)  38.9 us
    scatter x1, local copies, waits for them, and re-layouts, body(): outgoing = outgoing.at[targets, slot_pos[:, None]].set(payload)  19.7 us
    all_gather x1, blocking collectives, body(): piece = lax.all_gather(key_value, 'expert', axis=1, tiled=True)  16.8 us
  transfers between devices with their start and end apart: 4, of which 4 were waited for; matrix products, arithmetic and copies ran while one was open for 3% of the time, Pallas kernels for 0%

commit v1 on v0

--- a/solution.py
+++ b/solution.py
@@ -1,6 +1,10 @@
+import functools
+
 import jax
 import jax.numpy as jnp
 from jax import lax
+from jax.experimental import pallas as pl
+from jax.experimental.pallas import tpu as pltpu
 from jax.sharding import PartitionSpec as P
 
 FF = 6144
@@ -29,8 +33,10 @@
     one_hot = (route_flat[:, None] == jnp.arange(EXPERTS, dtype=jnp.int32)[None, :]).astype(
         jnp.int32
     )
-    earlier = jnp.cumsum(one_hot, axis=0) - one_hot
-    earlier_count = jnp.sum(earlier * one_hot, axis=1)
+    order = jnp.arange(route_flat.shape[0], dtype=jnp.int32)
+    before = (order[None, :] < order[:, None]).astype(jnp.bfloat16)
+    earlier = jnp.dot(before, one_hot.astype(jnp.bfloat16), preferred_element_type=jnp.float32)
+    earlier_count = jnp.sum(earlier.astype(jnp.int32) * one_hot, axis=1)
     slot_pos = route_flat % per_index * block_slots + earlier_count
     targets = (
         route_flat[:, None] * copies + jnp.arange(copies, dtype=jnp.int32)[None, :]
@@ -48,7 +54,7 @@
     return (jax.nn.silu(gate_vals) * up_vals * keep_mask).astype(jnp.bfloat16)
 
 
-def body(
+def plain_body(
     hidden,
     modulation,
     router_weight,
@@ -94,12 +100,12 @@
     picked = jnp.take_along_axis(logits, flat_ids, axis=1)
     first_weight = jax.nn.sigmoid(picked[:, 0] - picked[:, 1])
     route_weight = jnp.stack([first_weight, 1.0 - first_weight], axis=1)
-    route_count = row_count * TOP
-    route_token = jnp.arange(route_count, dtype=jnp.int32) // TOP
     targets, slot_pos = route_slots(flat_ids, block_slots, per_index, copies)
-    outgoing = jnp.zeros((experts_axis, slot_count, width), jnp.bfloat16)
-    payload = jnp.broadcast_to(flat_rows[route_token][:, None, :], (route_count, copies, width))
-    outgoing = outgoing.at[targets, slot_pos[:, None]].set(payload)
+    flat_place = (targets * slot_count + slot_pos[:, None]).reshape(row_count, TOP * copies)
+    all_places = jnp.arange(experts_axis * slot_count, dtype=jnp.int32)
+    chosen = jnp.any(all_places[:, None, None] == flat_place[None], axis=2).astype(jnp.bfloat16)
+    outgoing = jnp.dot(chosen, flat_rows, preferred_element_type=jnp.float32)
+    outgoing = outgoing.astype(jnp.bfloat16).reshape(experts_axis, slot_count, width)
     received = lax.all_to_all(outgoing, "expert", split_axis=0, concat_axis=0, tiled=True)
     received_rows = received.reshape(experts_axis * slot_count, width)
     piece = lax.all_gather(received_rows, ("dp", "head"), axis=0, tiled=True)
@@ -165,6 +171,378 @@
     return latent + step_size[:, None, None] * guided
 
 
+WEIGHT_SLOTS = 3
+MESH = pl.DeviceIdType.MESH
+
+
+def flipped(value, mask, bits):
+    total = 0
+    for bit in range(bits):
+        digit = lax.rem(lax.div(value, jnp.int32(2**bit)), jnp.int32(2))
+        if (mask >> bit) & 1:
+            digit = 1 - digit
+        total = total + digit * 2**bit
+    return total
+
+
+def slot_mask(slot):
+    return (slot & 3) | ((slot & 4) << 1) | ((slot & 8) >> 1)
+
+
+def fused_kernel(
+    cap,
+    tile,
+    hidden_ref,
+    modulation_ref,
+    router_ref,
+    ids_ref,
+    slots_ref,
+    slots_t_ref,
+    qkv_ref,
+    guide_out_ref,
+    main_final_ref,
+    guide_final_ref,
+    latent_ref,
+    guidance_ref,
+    step_ref,
+    gate_hbm,
+    up_hbm,
+    down_hbm,
+    out_ref,
+    outgoing,
+    recv,
+    result,
+    back,
+    total,
+    kv,
+    mix_own,
+    mix_send,
+    mix_recv,
+    gate_buf,
+    up_buf,
+    down_buf,
+    weight_sem,
+    go_send,
+    go_recv,
+    back_send,
+    back_recv,
+    kv_send,
+    kv_recv,
+    pair_send,
+    pair_recv,
+):
+    f32, bf16 = jnp.float32, jnp.bfloat16
+    tokens, width = hidden_ref.shape
+    heads, queries_dev, _ = qkv_ref.shape
+    units = gate_hbm.shape[1]
+    tiles = units // tile
+    half = EXPERTS // 2
+    half_rows = half * cap
+    my_z, my_x, my_core = lax.axis_index("expert"), lax.axis_index("dp"), lax.axis_index("head")
+
+    def device(mask):
+        return {
+            "expert": flipped(my_z, mask >> 2, 2),
+            "dp": flipped(my_x, (mask >> 1) & 1, 1),
+            "head": flipped(my_core, mask & 1, 1),
+        }
+
+    barrier = pltpu.get_barrier_semaphore()
+    for mask in range(1, EXPERTS):
+        pl.semaphore_signal(barrier, inc=1, device_id=device(mask), device_id_type=MESH)
+
+    def weight_copies(step):
+        slot = lax.rem(step, jnp.int32(WEIGHT_SLOTS))
+        start = pl.multiple_of(lax.rem(step, jnp.int32(tiles)) * tile, tile)
+        cols = pl.ds(start, tile)
+        return (
+            pltpu.make_async_copy(gate_hbm.at[:, cols], gate_buf.at[slot], weight_sem.at[0, slot]),
+            pltpu.make_async_copy(up_hbm.at[:, cols], up_buf.at[slot], weight_sem.at[1, slot]),
+            pltpu.make_async_copy(down_hbm.at[cols, :], down_buf.at[slot], weight_sem.at[2, slot]),
+        )
+
+    for step in range(WEIGHT_SLOTS - 1):
+        for copy in weight_copies(jnp.int32(step)):
+            copy.start()
+
+    for h in range(heads):
+        keys = unit_rows(qkv_ref[h, :, HD : 2 * HD].astype(f32)).astype(bf16)
+        kv[0, h] = jnp.concatenate([keys, qkv_ref[h, :, 2 * HD :]], axis=-1)
+
+    hidden_float = hidden_ref[...].astype(f32)
+    modulated = (
+        layer_norm(hidden_float) * (1.0 + modulation_ref[1:2, :]) + modulation_ref[0:1, :]
+    ).astype(bf16)
+
+    slot_row = slots_t_ref[...]
+    kind = lax.broadcasted_iota(jnp.int32, (EXPERTS, tokens), 0)
+    first_t = kind == slot_row[0:1, :]
+    second_t = kind == slot_row[1:2, :]
+    named_t = jnp.where(first_t | second_t, 1.0, 0.0).astype(bf16)
+    row = lax.broadcasted_iota(jnp.int32, (tokens, tokens), 0)
+    col = lax.broadcasted_iota(jnp.int32, (tokens, tokens), 1)
+    earlier_t = jnp.dot(
+        named_t, jnp.where(row < col, 1.0, 0.0).astype(bf16), preferred_element_type=f32
+    )
+    place_t = [
+        slot_row[k : k + 1, :] * cap
+        + jnp.sum(jnp.where(hot, earlier_t, 0.0), axis=0, keepdims=True).astype(jnp.int32)
+        for k, hot in enumerate((first_t, second_t))
+    ]
+    for part in range(2):
+        place = lax.broadcasted_iota(jnp.int32, (half_rows, tokens), 0) + part * half_rows
+        chosen = jnp.where((place == place_t[0]) | (place == place_t[1]), 1.0, 0.0).astype(bf16)
+        rows = jnp.dot(chosen, modulated, preferred_element_type=f32).astype(bf16)
+        outgoing[pl.ds(part * half_rows, half_rows), :] = rows
+        if part == 0:
+            recv[pl.ds(0, cap), :] = rows[:cap]
+
+    pl.semaphore_wait(barrier, EXPERTS - 1)
+
+    kv_copies = []
+    for j in range(1, kv.shape[0]):
+        kv_copies.append(
+            pltpu.make_async_remote_copy(
+                src_ref=kv.at[0],
+                dst_ref=kv.at[j],
+                send_sem=kv_send.at[j],
+                recv_sem=kv_recv.at[j],
+                device_id=device(j << 2),
+                device_id_type=MESH,
+            )
+        )
+        kv_copies[-1].start()
+
+    def row_copy(source, target, send_sem, recv_sem, slot):
+        rows = pl.ds(slot * cap, cap)
+        return pltpu.make_async_remote_copy(
+            src_ref=source.at[rows, :],
+            dst_ref=target.at[rows, :],
+            send_sem=send_sem.at[slot],
+            recv_sem=recv_sem.at[slot],
+            device_id=device(slot_mask(slot)),
+            device_id_type=MESH,
+        )
+
+    order = [[4, 5, 6, 7, 1, 2, 3], [12, 13, 14, 15, 8, 9, 10, 11]]
+    go, home = {}, {}
+    for part in range(2):
+        for slot in order[part]:
+            go[slot] = row_copy(outgoing, recv, go_send, go_recv, slot)
+            go[slot].start()
+
+    logits = jnp.dot(
+        modulated.astype(f32), router_ref[...], precision=lax.Precision.HIGHEST,
+        preferred_element_type=f32,
+    )
+    lane = lax.broadcasted_iota(jnp.int32, (tokens, EXPERTS), 1)
+    ids = ids_ref[...]
+    picked = [
+        jnp.sum(jnp.where(lane == ids[:, k : k + 1], logits, 0.0), axis=1, keepdims=True)
+        for k in range(TOP)
+    ]
+    first_weight = 1.0 / (1.0 + jnp.exp(picked[1] - picked[0]))
+    route_weight = [first_weight, 1.0 - first_weight]
+    slots = slots_ref[...]
+    hot = [lane == slots[:, k : k + 1] for k in range(TOP)]
+    earlier = jnp.dot(
+        jnp.where(col < row, 1.0, 0.0).astype(bf16),
+        jnp.where(hot[0] | hot[1], 1.0, 0.0).astype(bf16),
+        preferred_element_type=f32,
+    )
+    places = [
+        slots[:, k : k + 1] * cap
+        + jnp.sum(jnp.where(hot[k], earlier, 0.0), axis=1, keepdims=True).astype(jnp.int32)
+        for k in range(TOP)
+    ]
+
+    for copy in kv_copies:
+        copy.wait_recv()
+    mix = jnp.zeros((queries_dev, guide_out_ref.shape[-1]), f32)
+    for h in range(heads):
+        queries = unit_rows(qkv_ref[h, :, :HD].astype(f32)).astype(bf16)
+        weight_total = jnp.zeros((queries_dev, 1), f32)
+        weighted = jnp.zeros((queries_dev, HD), f32)
+        for j in range(kv.shape[0]):
+            scores = lax.dot_general(
+                queries, kv[j, h, :, :HD], (((1,), (1,)), ((), ())), preferred_element_type=f32
+            ) * (score_scale / HD)
+            weights = jnp.exp(scores - score_scale)
+            weight_total = weight_total + jnp.sum(weights, axis=-1, keepdims=True)
+            weighted = weighted + jnp.dot(
+                weights.astype(bf16), kv[j, h, :, HD:], preferred_element_type=f32
+            )
+        attended = (weighted / weight_total).astype(bf16)
+        mix = mix + jnp.dot(attended, guide_out_ref[h], preferred_element_type=f32)
+    mix = mix.reshape(2, tokens, mix.shape[-1])
+    mix_own[...] = mix
+    mix_send[...] = mix.astype(bf16)
+    pair = pltpu.make_async_remote_copy(
+        src_ref=mix_send.at[1 - my_core],
+        dst_ref=mix_recv,
+        send_sem=pair_send,
+        recv_sem=pair_recv,
+        device_id=device(1),
+        device_id_type=MESH,
+    )
+    pair.start()
+
+    for part in range(2):
+        for slot in order[part]:
+            go[slot].wait_recv()
+        total[...] = jnp.zeros_like(total)
+
+        def expert_step(t, carry, part=part):
+            step = t + part * tiles
+            slot = lax.rem(step, jnp.int32(WEIGHT_SLOTS))
+
+            @pl.when(step + (WEIGHT_SLOTS - 1) < 2 * tiles)
+            def _():
+                for copy in weight_copies(step + (WEIGHT_SLOTS - 1)):
+                    copy.start()
+
+            for copy in weight_copies(step):
+                copy.wait()
+            rows = recv[pl.ds(part * half_rows, half_rows), :]
+            gate_vals = jnp.dot(rows, gate_buf[slot], preferred_element_type=f32)
+            up_vals = jnp.dot(rows, up_buf[slot], preferred_element_type=f32)
+            activated = (gate_vals / (1.0 + jnp.exp(-gate_vals)) * up_vals).astype(bf16)
+            total[...] += jnp.dot(activated, down_buf[slot], preferred_element_type=f32)
+            return carry
+
+        lax.fori_loop(jnp.int32(0), jnp.int32(tiles), expert_step, jnp.int32(0))
+        result[pl.ds(part * half_rows, half_rows), :] = total[...].astype(bf16)
+        for slot in order[part]:
+            home[slot] = row_copy(result, back, back_send, back_recv, slot)
+            home[slot].start()
+        if part == 0:
+            back[pl.ds(0, cap), :] = result[pl.ds(0, cap), :]
+
+    pair.wait_recv()
+    guide_norm = layer_norm(mix_own[my_core] + mix_recv[...].astype(f32)).astype(bf16)
+    guide_velocity = jnp.dot(guide_norm, guide_final_ref[...], preferred_element_type=f32)
+
+    moe = jnp.zeros((tokens, width), f32)
+    for part in range(2):
+        for slot in order[part]:
+            home[slot].wait_recv()
+        returned = back[pl.ds(part * half_rows, half_rows), :]
+        place = lax.broadcasted_iota(jnp.int32, (tokens, half_rows), 1) + part * half_rows
+        for k in range(TOP):
+            chosen = jnp.where(place == places[k], 1.0, 0.0).astype(bf16)
+            moe = moe + route_weight[k] * jnp.dot(chosen, returned, preferred_element_type=f32)
+    updated = hidden_ref[...].astype(f32) + modulation_ref[2:3, :] * moe
+    main_norm = layer_norm(updated).astype(bf16)
+    main_velocity = jnp.dot(main_norm, main_final_ref[...], preferred_element_type=f32)
+    guided = guide_velocity + guidance_ref[...] * (main_velocity - guide_velocity)
+    out_ref[...] = latent_ref[...] + step_ref[...] * guided
+
+    for copy in kv_copies:
+        copy.wait_send()
+    for copies in (go, home):
+        for slot in order[0] + order[1]:
+            copies[slot].wait_send()
+    pair.wait_send()
+
+
+def fused_body(
+    hidden,
+    modulation,
+    router_weight,
+    route_ids,
+    gate_weight,
+    up_weight,
+    down_weight,
+    main_final,
+    guide_qkv,
+    guide_out,
+    guide_final,
+    latent,
+    guidance,
+    step_size,
+):
+    _, tokens, width = hidden.shape
+    units = gate_weight.shape[1]
+    cap = 2 * tokens * TOP // EXPERTS
+    z_size = lax.axis_size("expert")
+    tile = 512
+    heads = guide_qkv.shape[2]
+    queries_dev = guide_qkv.shape[1]
+    guide_width = guide_out.shape[-1]
+    ids = route_ids[0]
+    slots = slot_mask(ids ^ lax.axis_index(("expert", "dp", "head")))
+    qkv = jnp.transpose(guide_qkv[0], (1, 0, 2))
+    vmem = pl.BlockSpec(memory_space=pltpu.VMEM)
+    hbm = pl.BlockSpec(memory_space=pl.ANY)
+    bf16, f32 = jnp.bfloat16, jnp.float32
+    dma = pltpu.SemaphoreType.DMA
+    row_total = EXPERTS * cap
+    out = pl.pallas_call(
+        functools.partial(fused_kernel, cap, tile),
+        out_shape=jax.ShapeDtypeStruct((tokens, P_SIZE), f32),
+        in_specs=[vmem] * 13 + [hbm] * 3,
+        out_specs=vmem,
+        scratch_shapes=[
+            pltpu.VMEM((row_total, width), bf16),
+            pltpu.VMEM((row_total, width), bf16),
+            pltpu.VMEM((row_total, width), bf16),
+            pltpu.VMEM((row_total, width), bf16),
+            pltpu.VMEM((row_total // 2, width), f32),
+            pltpu.VMEM((z_size, heads, queries_dev, 2 * HD), bf16),
+            pltpu.VMEM((2, tokens, guide_width), f32),
+            pltpu.VMEM((2, tokens, guide_width), bf16),
+            pltpu.VMEM((tokens, guide_width), bf16),
+            pltpu.VMEM((WEIGHT_SLOTS, width, tile), bf16),
+            pltpu.VMEM((WEIGHT_SLOTS, width, tile), bf16),
+            pltpu.VMEM((WEIGHT_SLOTS, tile, width), bf16),
+            dma((3, WEIGHT_SLOTS)),
+            dma((EXPERTS,)),
+            dma((EXPERTS,)),
+            dma((EXPERTS,)),
+            dma((EXPERTS,)),
+            dma((z_size,)),
+            dma((z_size,)),
+            dma,
+            dma,
+        ],
+        compiler_params=pltpu.CompilerParams(
+            collective_id=0, has_side_effects=True, vmem_limit_bytes=50 * 2**20
+        ),
+        cost_estimate=pl.CostEstimate(
+            flops=6 * row_total * width * units,
+            bytes_accessed=12 * width * units,
+            transcendentals=row_total * units,
+        ),
+    )(
+        hidden[0],
+        modulation[0],
+        router_weight,
+        ids,
+        slots,
+        slots.T,
+        qkv,
+        guide_out,
+        main_final,
+        guide_final,
+        latent[0],
+        guidance[:, None],
+        step_size[:, None],
+        gate_weight,
+        up_weight,
+        down_weight,
+    )
+    return out[None]
+
+
+def body(*arrays):
+    hidden, gate_weight, guide_qkv = arrays[0], arrays[4], arrays[8]
+    sizes = [lax.axis_size(name) for name in ("expert", "dp", "head")]
+    whole_experts = gate_weight.shape[1] == FF and sizes == [4, 2, 2]
+    if whole_experts and hidden.shape[0] == 1 and hidden.shape[1] % 128 == 0:
+        return fused_body(*arrays)
+    return plain_body(*arrays)
+
+
 def solution(mesh):
     in_specs = (
         P(("groups", "dp"), ("expert", "head"), None),

time: 397 us -> 118 us (0.30); the launches traced: 391 us -> 117 us
  matrix products: 159 us -> 0 us
  waiting for transfers between devices: 108 us -> 0 us
  Pallas kernels: 0 us -> 106 us
  blocking collectives: 55.7 us -> 0 us
  local copies, waits for them, and re-layouts: 32.5 us -> 9.13 us
  between operations: 16.5 us -> 1.34 us
  other arithmetic: 14 us -> 1.37 us
  starting transfers between devices: 4.63 us -> 0 us
    dot_general x8 -> x0, matrix products: 159 us -> none  [the longest x1 55.4 us: expert_hidden(): up_vals = jnp.dot(rows, up_weight, preferred_element_type=jnp.float32)]
    pallas_call x0 -> x1, Pallas kernels: none -> 106 us  [fused_body(): pl.pallas_call(functools.partial(fused_kernel, cap, tile), out_shape=jax....]
    all_gather x1 -> x0, waiting for transfers between devices: 48.7 us -> none  [body(): piece = lax.all_gather(received_rows, ('dp', 'head'), axis=0, tiled=True)]
    reduce_scatter x2 -> x0, waiting for transfers between devices: 44.5 us -> none  [the longest x1 40.2 us: body(): lax.psum_scatter(lax.optimization_barrier(term.astype(jnp.bfloat16)).asty...]
    all_to_all x1 -> x0, blocking collectives: 38.9 us -> none  [body(): lax.all_to_all(outgoing, 'expert', split_axis=0, concat_axis=0, tiled=True)]
    scatter x1 -> x0, local copies, waits for them, and re-layouts: 19.7 us -> none  [body(): outgoing = outgoing.at[targets, slot_pos[:, None]].set(payload)]
    all_gather x1 -> x0, blocking collectives: 16.8 us -> none  [body(): piece = lax.all_gather(key_value, 'expert', axis=1, tiled=True)]
    all_to_all x1 -> x0, waiting for transfers between devices: 14.9 us -> none  [body(): lax.all_to_all(row_sums.reshape(experts_axis, slot_count, width).astype(j...]
  transfers between devices with their start and end apart: 4 -> 0, of which waited for: 4 -> 0; matrix products, arithmetic and copies ran while one was open for 3% -> 0% of each run, Pallas kernels for 0% -> 0%
where the time goes in v1:
time: 118 us; the launch traced here: 117 us
  Pallas kernels  106 us (90%)
  local copies, waits for them, and re-layouts  9.13 us (8%)
  other arithmetic  1.37 us (1%)
  between operations  1.34 us (1%)
    pallas_call x1, Pallas kernels, fused_body(): pl.pallas_call(functools.partial(fused_kernel, cap, tile), out_shape=jax....  106 us
    unnamed x10, local copies, waits for them, and re-layouts  7.56 us

profile of v1, /device:TPU:13, one launch (start us, length us, event | category | flops | bytes accessed | tf_op | source)
XLA Modules:
  0.0 117.5 jit_solution(6205681638084326847)
XLA Ops:
  1.3 0.7 fusion.slots_t_ref
  2.0 0.7 shift-right-arithmetic_or_fusion
  2.7 0.7 copy.25
  3.4 0.1 copy.19.slots_ref
  3.5 0.8 copy.16
  4.3 0.8 copy.18.ids_ref
  5.1 0.8 copy.21.guide_final_ref
  5.9 1.0 copy.20.main_final_ref
  7.0 1.1 copy.15
  8.1 1.2 copy.17.router_ref
  9.3 0.0 copy-start
  9.3 1.0 copy-done
  10.3 0.0 copy-start.1
  10.3 0.9 copy-done.1
  11.2 105.6 %shard_map.136 = f32[128,16]{1,0:T(8,128)S(1)} custom-call(bf16[128,1536]{1,0:T(8,128)(2,1)S(1)} %bitcast.23, f32[3,1536]{1,0:T(4,128)S(1)} %bitcast.22, f32[1536,16]{1,0:T(8,128)S(1)} %copy.17.router_ref, s32[128,2]{1,0:T(8,128)S(1)} %copy.18.ids_ref, s32[128,2]{1,0:T(8,128)S(1)} %copy.19.slots_ref, s32[2,128]{1,0:T(2,128)S(1)} %fusion.slots_t_ref, ...), custom_call_target="tpu_custom_call" | custom-call | flops 28991029248 | bytes 113246208 | tf_op jit(solution)/shard_map/pallas_call | solution.py:480
  116.8 0.7 copy.22
Async XLA Ops:
  9.3 1.0 copy-start
  10.3 0.9 copy-start.1

commit v2 on v1

--- a/solution.py
+++ b/solution.py
@@ -185,6 +185,10 @@
     return total
 
 
+def unit_columns(values):
+    return values / jnp.sqrt(jnp.mean(values * values, axis=0, keepdims=True) + epsilon)
+
+
 def slot_mask(slot):
     return (slot & 3) | ((slot & 4) << 1) | ((slot & 8) >> 1)
 
@@ -195,8 +199,7 @@
     hidden_ref,
     modulation_ref,
     router_ref,
-    ids_ref,
-    slots_ref,
+    ids_t_ref,
     slots_t_ref,
     qkv_ref,
     guide_out_ref,
@@ -233,7 +236,7 @@
 ):
     f32, bf16 = jnp.float32, jnp.bfloat16
     tokens, width = hidden_ref.shape
-    heads, queries_dev, _ = qkv_ref.shape
+    heads, _, queries_dev = qkv_ref.shape
     units = gate_hbm.shape[1]
     tiles = units // tile
     half = EXPERTS // 2
@@ -266,12 +269,12 @@
             copy.start()
 
     for h in range(heads):
-        keys = unit_rows(qkv_ref[h, :, HD : 2 * HD].astype(f32)).astype(bf16)
-        kv[0, h] = jnp.concatenate([keys, qkv_ref[h, :, 2 * HD :]], axis=-1)
+        kv[my_z, h, :HD] = unit_columns(qkv_ref[h, HD : 2 * HD].astype(f32)).astype(bf16)
+        kv[my_z, h, HD:] = qkv_ref[h, 2 * HD :]
 
     hidden_float = hidden_ref[...].astype(f32)
     modulated = (
-        layer_norm(hidden_float) * (1.0 + modulation_ref[1:2, :]) + modulation_ref[0:1, :]
+        layer_norm(hidden_float) * (1.0 + modulation_ref[1]) + modulation_ref[0]
     ).astype(bf16)
 
     slot_row = slots_t_ref[...]
@@ -299,19 +302,26 @@
 
     pl.semaphore_wait(barrier, EXPERTS - 1)
 
-    kv_copies = []
-    for j in range(1, kv.shape[0]):
-        kv_copies.append(
-            pltpu.make_async_remote_copy(
-                src_ref=kv.at[0],
-                dst_ref=kv.at[j],
-                send_sem=kv_send.at[j],
-                recv_sem=kv_recv.at[j],
-                device_id=device(j << 2),
-                device_id_type=MESH,
-            )
+    in_middle = jnp.logical_or(my_z == 1, my_z == 2)
+
+    def kv_copy(owner_mask, target_mask, send, receive):
+        block = flipped(my_z, owner_mask, 2)
+        return pltpu.make_async_remote_copy(
+            src_ref=kv.at[block],
+            dst_ref=kv.at[block],
+            send_sem=kv_send.at[send],
+            recv_sem=kv_recv.at[receive],
+            device_id=device(target_mask << 2),
+            device_id_type=MESH,
         )
-        kv_copies[-1].start()
+
+    kv_near = kv_copy(0, 1, 0, 0)
+    kv_own_over = kv_copy(0, 3, 1, 1)
+    kv_near_over = kv_copy(1, 3, 2, 2)
+    kv_own_on = kv_copy(3, 1, 3, 1)
+    kv_near_on = kv_copy(2, 1, 4, 2)
+    kv_near.start()
+    pl.when(in_middle)(kv_own_over.start)
 
     def row_copy(source, target, send_sem, recv_sem, slot):
         rows = pl.ds(slot * cap, cap)
@@ -331,49 +341,91 @@
             go[slot] = row_copy(outgoing, recv, go_send, go_recv, slot)
             go[slot].start()
 
-    logits = jnp.dot(
-        modulated.astype(f32), router_ref[...], precision=lax.Precision.HIGHEST,
+    logits = lax.dot_general(
+        router_ref[...],
+        modulated.astype(f32),
+        (((1,), (1,)), ((), ())),
+        precision=lax.Precision.HIGHEST,
         preferred_element_type=f32,
     )
-    lane = lax.broadcasted_iota(jnp.int32, (tokens, EXPERTS), 1)
-    ids = ids_ref[...]
+    ids_t = ids_t_ref[...]
     picked = [
-        jnp.sum(jnp.where(lane == ids[:, k : k + 1], logits, 0.0), axis=1, keepdims=True)
+        jnp.sum(jnp.where(kind == ids_t[k : k + 1, :], logits, 0.0), axis=0, keepdims=True)
         for k in range(TOP)
     ]
-    first_weight = 1.0 / (1.0 + jnp.exp(picked[1] - picked[0]))
+
+    def as_column(values):
+        return jnp.sum(jnp.where(row == col, values, 0.0), axis=1, keepdims=True)
+
+    first_weight = as_column(1.0 / (1.0 + jnp.exp(picked[1] - picked[0])))
     route_weight = [first_weight, 1.0 - first_weight]
-    slots = slots_ref[...]
-    hot = [lane == slots[:, k : k + 1] for k in range(TOP)]
-    earlier = jnp.dot(
-        jnp.where(col < row, 1.0, 0.0).astype(bf16),
-        jnp.where(hot[0] | hot[1], 1.0, 0.0).astype(bf16),
-        preferred_element_type=f32,
-    )
-    places = [
-        slots[:, k : k + 1] * cap
-        + jnp.sum(jnp.where(hot[k], earlier, 0.0), axis=1, keepdims=True).astype(jnp.int32)
-        for k in range(TOP)
-    ]
-
-    for copy in kv_copies:
-        copy.wait_recv()
+    places = [as_column(place.astype(f32)).astype(jnp.int32) for place in place_t]
+
+    kv_near.wait_recv()
+    pl.when(in_middle)(kv_near_over.start)
+
+    for part in range(2):
+        for slot in order[part]:
+            go[slot].wait_recv()
+        total[...] = jnp.zeros_like(total)
+
+        def expert_step(t, carry, part=part):
+            step = t + part * tiles
+            slot = lax.rem(step, jnp.int32(WEIGHT_SLOTS))
+
+            @pl.when(step + (WEIGHT_SLOTS - 1) < 2 * tiles)
+            def _():
+                for copy in weight_copies(step + (WEIGHT_SLOTS - 1)):
+                    copy.start()
+
+            for copy in weight_copies(step):
+                copy.wait()
+            rows = recv[pl.ds(part * half_rows, half_rows), :]
+            gate_vals = jnp.dot(rows, gate_buf[slot], preferred_element_type=f32)
+            up_vals = jnp.dot(rows, up_buf[slot], preferred_element_type=f32)
+            activated = (gate_vals / (1.0 + jnp.exp(-gate_vals)) * up_vals).astype(bf16)
+            total[...] += jnp.dot(activated, down_buf[slot], preferred_element_type=f32)
+            return carry
+
+        lax.fori_loop(jnp.int32(0), jnp.int32(tiles), expert_step, jnp.int32(0))
+        result[pl.ds(part * half_rows, half_rows), :] = total[...].astype(bf16)
+        for slot in order[part]:
+            home[slot] = row_copy(result, back, back_send, back_recv, slot)
+            home[slot].start()
+        if part == 0:
+            back[pl.ds(0, cap), :] = result[pl.ds(0, cap), :]
+
+            @pl.when(in_middle)
+            def _():
+                kv_own_over.wait_recv()
+                kv_own_on.start()
+                kv_near_over.wait_recv()
+                kv_near_on.start()
+
+
+    @pl.when(jnp.logical_not(in_middle))
+    def _():
+        kv_own_over.wait_recv()
+        kv_near_over.wait_recv()
+
     mix = jnp.zeros((queries_dev, guide_out_ref.shape[-1]), f32)
     for h in range(heads):
-        queries = unit_rows(qkv_ref[h, :, :HD].astype(f32)).astype(bf16)
-        weight_total = jnp.zeros((queries_dev, 1), f32)
-        weighted = jnp.zeros((queries_dev, HD), f32)
+        queries = unit_columns(qkv_ref[h, :HD].astype(f32)).astype(bf16)
+        weight_total = jnp.zeros((1, queries_dev), f32)
+        weighted = jnp.zeros((HD, queries_dev), f32)
         for j in range(kv.shape[0]):
             scores = lax.dot_general(
-                queries, kv[j, h, :, :HD], (((1,), (1,)), ((), ())), preferred_element_type=f32
+                kv[j, h, :HD], queries, (((0,), (0,)), ((), ())), preferred_element_type=f32
             ) * (score_scale / HD)
             weights = jnp.exp(scores - score_scale)
-            weight_total = weight_total + jnp.sum(weights, axis=-1, keepdims=True)
+            weight_total = weight_total + jnp.sum(weights, axis=0, keepdims=True)
             weighted = weighted + jnp.dot(
-                weights.astype(bf16), kv[j, h, :, HD:], preferred_element_type=f32
+                kv[j, h, HD:], weights.astype(bf16), preferred_element_type=f32
             )
         attended = (weighted / weight_total).astype(bf16)
-        mix = mix + jnp.dot(attended, guide_out_ref[h], preferred_element_type=f32)
+        mix = mix + lax.dot_general(
+            attended, guide_out_ref[h], (((0,), (0,)), ((), ())), preferred_element_type=f32
+        )
     mix = mix.reshape(2, tokens, mix.shape[-1])
     mix_own[...] = mix
     mix_send[...] = mix.astype(bf16)
@@ -387,40 +439,11 @@
     )
     pair.start()
 
-    for part in range(2):
-        for slot in order[part]:
-            go[slot].wait_recv()
-        total[...] = jnp.zeros_like(total)
-
-        def expert_step(t, carry, part=part):
-            step = t + part * tiles
-            slot = lax.rem(step, jnp.int32(WEIGHT_SLOTS))
-
-            @pl.when(step + (WEIGHT_SLOTS - 1) < 2 * tiles)
-            def _():
-                for copy in weight_copies(step + (WEIGHT_SLOTS - 1)):
-                    copy.start()
-
-            for copy in weight_copies(step):
-                copy.wait()
-            rows = recv[pl.ds(part * half_rows, half_rows), :]
-            gate_vals = jnp.dot(rows, gate_buf[slot], preferred_element_type=f32)
-            up_vals = jnp.dot(rows, up_buf[slot], preferred_element_type=f32)
-            activated = (gate_vals / (1.0 + jnp.exp(-gate_vals)) * up_vals).astype(bf16)
-            total[...] += jnp.dot(activated, down_buf[slot], preferred_element_type=f32)
-            return carry
-
-        lax.fori_loop(jnp.int32(0), jnp.int32(tiles), expert_step, jnp.int32(0))
-        result[pl.ds(part * half_rows, half_rows), :] = total[...].astype(bf16)
-        for slot in order[part]:
-            home[slot] = row_copy(result, back, back_send, back_recv, slot)
-            home[slot].start()
-        if part == 0:
-            back[pl.ds(0, cap), :] = result[pl.ds(0, cap), :]
-
     pair.wait_recv()
     guide_norm = layer_norm(mix_own[my_core] + mix_recv[...].astype(f32)).astype(bf16)
-    guide_velocity = jnp.dot(guide_norm, guide_final_ref[...], preferred_element_type=f32)
+    guide_velocity = lax.dot_general(
+        guide_final_ref[...], guide_norm, (((1,), (1,)), ((), ())), preferred_element_type=f32
+    )
 
     moe = jnp.zeros((tokens, width), f32)
     for part in range(2):
@@ -431,14 +454,21 @@
         for k in range(TOP):
             chosen = jnp.where(place == places[k], 1.0, 0.0).astype(bf16)
             moe = moe + route_weight[k] * jnp.dot(chosen, returned, preferred_element_type=f32)
-    updated = hidden_ref[...].astype(f32) + modulation_ref[2:3, :] * moe
+    updated = hidden_ref[...].astype(f32) + modulation_ref[2] * moe
     main_norm = layer_norm(updated).astype(bf16)
-    main_velocity = jnp.dot(main_norm, main_final_ref[...], preferred_element_type=f32)
+    main_velocity = lax.dot_general(
+        main_final_ref[...], main_norm, (((1,), (1,)), ((), ())), preferred_element_type=f32
+    )
     guided = guide_velocity + guidance_ref[...] * (main_velocity - guide_velocity)
     out_ref[...] = latent_ref[...] + step_ref[...] * guided
 
-    for copy in kv_copies:
-        copy.wait_send()
+    kv_near.wait_send()
+
+    @pl.when(in_middle)
+    def _():
+        for copy in (kv_own_over, kv_near_over, kv_own_on, kv_near_on):
+            copy.wait_send()
+
     for copies in (go, home):
         for slot in order[0] + order[1]:
             copies[slot].wait_send()
@@ -469,9 +499,9 @@
     heads = guide_qkv.shape[2]
     queries_dev = guide_qkv.shape[1]
     guide_width = guide_out.shape[-1]
-    ids = route_ids[0]
-    slots = slot_mask(ids ^ lax.axis_index(("expert", "dp", "head")))
-    qkv = jnp.transpose(guide_qkv[0], (1, 0, 2))
+    ids_t = route_ids[0].T
+    slots_t = slot_mask(ids_t ^ lax.axis_index(("expert", "dp", "head")))
+    qkv = jnp.transpose(guide_qkv[0], (1, 2, 0))
     vmem = pl.BlockSpec(memory_space=pltpu.VMEM)
     hbm = pl.BlockSpec(memory_space=pl.ANY)
     bf16, f32 = jnp.bfloat16, jnp.float32
@@ -479,8 +509,8 @@
     row_total = EXPERTS * cap
     out = pl.pallas_call(
         functools.partial(fused_kernel, cap, tile),
-        out_shape=jax.ShapeDtypeStruct((tokens, P_SIZE), f32),
-        in_specs=[vmem] * 13 + [hbm] * 3,
+        out_shape=jax.ShapeDtypeStruct((P_SIZE, tokens), f32),
+        in_specs=[vmem] * 12 + [hbm] * 3,
         out_specs=vmem,
         scratch_shapes=[
             pltpu.VMEM((row_total, width), bf16),
@@ -488,7 +518,7 @@
             pltpu.VMEM((row_total, width), bf16),
             pltpu.VMEM((row_total, width), bf16),
             pltpu.VMEM((row_total // 2, width), f32),
-            pltpu.VMEM((z_size, heads, queries_dev, 2 * HD), bf16),
+            pltpu.VMEM((z_size, heads, 2 * HD, queries_dev), bf16),
             pltpu.VMEM((2, tokens, guide_width), f32),
             pltpu.VMEM((2, tokens, guide_width), bf16),
             pltpu.VMEM((tokens, guide_width), bf16),
@@ -500,8 +530,8 @@
             dma((EXPERTS,)),
             dma((EXPERTS,)),
             dma((EXPERTS,)),
-            dma((z_size,)),
-            dma((z_size,)),
+            dma((5,)),
+            dma((3,)),
             dma,
             dma,
         ],
@@ -515,23 +545,22 @@
         ),
     )(
         hidden[0],
-        modulation[0],
-        router_weight,
-        ids,
-        slots,
-        slots.T,
+        jnp.transpose(modulation, (1, 0, 2)),
+        router_weight.T,
+        ids_t,
+        slots_t,
         qkv,
         guide_out,
-        main_final,
-        guide_final,
-        latent[0],
+        main_final.T,
+        guide_final.T,
+        latent[0].T,
         guidance[:, None],
         step_size[:, None],
         gate_weight,
         up_weight,
         down_weight,
     )
-    return out[None]
+    return out.T[None]
 
 
 def body(*arrays):

time: 118 us -> 104 us (0.88)
  Pallas kernels: 106 us -> 93.2 us
    pallas_call x1, Pallas kernels: 106 us -> 93.2 us  [fused_body(): pl.pallas_call(functools.partial(fused_kernel, cap, tile), out_shape=jax....]
    unnamed x10 -> x19, local copies, waits for them, and re-layouts: 7.56 us -> 7.96 us
where the time goes in v2:
time: 104 us; the launch traced here: 103 us
  Pallas kernels  93.2 us (90%)
  local copies, waits for them, and re-layouts  7.96 us (8%)
  between operations  1.32 us (1%)
    pallas_call x1, Pallas kernels, fused_body(): pl.pallas_call(functools.partial(fused_kernel, cap, tile), out_shape=jax....  93.2 us
    unnamed x19, local copies, waits for them, and re-layouts  7.96 us

profile of v2, /device:TPU:13, one launch (start us, length us, event | category | flops | bytes accessed | tf_op | source)
XLA Modules:
  0.0 103.1 jit_solution(9185068227979540879)
XLA Ops:
  1.3 0.7 shift-right-arithmetic_or_fusion.slots_t_ref
  2.0 0.0 copy-start
  2.0 0.7 copy-done
  2.7 0.0 copy-start.1
  2.7 1.0 copy-done.1
  3.7 0.0 copy-start.2
  3.7 1.0 copy-done.2
  4.6 0.0 copy-start.3
  4.6 0.9 copy-done.3
  5.5 0.0 copy-start.4
  5.5 0.9 copy-done.4
  6.4 0.0 copy-start.5
  6.4 0.8 copy-done.5
  7.2 0.0 copy-start.6
  7.2 0.7 copy-done.6
  7.9 0.0 copy-start.7
  8.0 0.7 copy-done.7
  8.7 0.0 copy-start.8
  8.7 0.7 copy-done.8
  9.4 93.2 %shard_map.136 = f32[16,128]{1,0:T(8,128)S(1)} custom-call(bf16[128,1536]{1,0:T(8,128)(2,1)S(1)} %bitcast.24, f32[3,1,1536]{2,1,0:T(1,128)S(1)} %bitcast.28, f32[16,1536]{1,0:T(8,128)S(1)} %bitcast.26, s32[2,128]{1,0:T(2,128)S(1)} %bitcast.23, s32[2,128]{1,0:T(2,128)S(1)} %shift-right-arithmetic_or_fusion.slots_t_ref, bf16[3,192,256]{2,1,0:T(8,128)(2,1)S(1)} %bitcast.25, ...), custom_call_target="tpu_custom_call" | custom-call | flops 28991029248 | bytes 113246208 | tf_op jit(solution)/shard_map/pallas_call | solution.py:510
  102.5 0.6 copy.18
Async XLA Ops:
  2.0 0.7 copy-start
  2.7 1.0 copy-start.1
  3.7 1.0 copy-start.2
  4.6 0.9 copy-start.3
  5.5 0.9 copy-start.4
  6.4 0.8 copy-start.5
  7.2 0.7 copy-start.6
  7.9 0.7 copy-start.7
  8.7 0.7 copy-start.8
